TPU v7x, 256 devices: a whole 4x4x8 slice. The times are simulated.
256 devices in a mesh: dp: 8 (over y, x_hi), tensor: 32 (over z, x_lo, core).
Axes of the slice: x: 4 (x_hi: 2, x_lo: 2; x = x_hi * 2 + x_lo), y: 4, z: 8, core: 2. Of those that a mesh axis runs over, the one named last changes fastest.
Arguments:
- tokens: bfloat16 [2048, 5120], P('dp', 'tensor'), may hold values from -6 to 6
- out_grad: bfloat16 [2048, 5120], P('dp', 'tensor'), may hold values from -6 to 6
- master: float32 [3, 12800, 5120], P(None, 'tensor', 'dp'), may hold values from -50 to 50
- moment_first: float32 [3, 12800, 5120], P(None, 'tensor', 'dp'), may hold values from -10 to 10
- moment_second: float32 [3, 12800, 5120], P(None, 'tensor', 'dp'), may hold values from 0.01 to 0.1
Outputs:
- token_grad: bfloat16 [2048, 5120], P('dp', 'tensor')
- scaled_step: float32 [3, 12800, 5120], P(None, 'tensor', 'dp')
All inputs are finite; a program needn't handle non-finite values.
Results may differ from a plain program's by a relative error of at most 0.029.
Values may be sent and summed in bfloat16 or wider, within the bound.
No kernel may reach another device: no remote copies, remote signals or barrier semaphores. Data moves between devices by JAX's collectives and lax.ppermute only.
A program may use at most 128 MiB of HBM per device.

v0:
```python
import jax
import jax.numpy as jnp
from jax import lax
from jax.sharding import PartitionSpec as P

D = 5120
FF = 12800
beta_first = 0.9
beta_second = 0.95
epsilon = 1e-06
weight_decay = 0.1
step_power = 3.0


def contract_last(left, right):
    return lax.dot_general(
        left, right, (((1,), (1,)), ((), ())), preferred_element_type=jnp.float32
    )


def contract_rows(left, right):
    return lax.dot_general(
        left, right, (((0,), (0,)), ((), ())), preferred_element_type=jnp.float32
    )


def local(tokens, out_grad, master, moment_first, moment_second):
    scale_in = D ** (-0.5)
    scale_out = FF ** (-0.5)
    width = master.shape[1]
    columns = master.shape[2]
    inputs, out_rows = (
        lax.all_gather(tokens, "tensor", axis=1, tiled=True),
        lax.all_gather(out_grad, "tensor", axis=1, tiled=True),
    )
    local_weights = master.astype(jnp.bfloat16)
    weights = lax.all_gather(local_weights, "dp", axis=2, tiled=True)
    paired_weights = weights[:2].reshape(2 * width, weights.shape[2])
    both_pre = scale_in * contract_last(inputs, paired_weights)
    gate_pre = both_pre[:, :width]
    up_pre = both_pre[:, width:]
    hid_grad = scale_out * contract_last(out_rows, weights[2])
    sigmoid_gate = jax.nn.sigmoid(gate_pre)
    swish_gate = gate_pre * sigmoid_gate
    hidden = (swish_gate * up_pre).astype(jnp.bfloat16)
    gate_grad = (hid_grad * up_pre * sigmoid_gate * (1.0 + gate_pre * (1.0 - sigmoid_gate))).astype(
        jnp.bfloat16
    )
    up_grad = (hid_grad * swish_gate).astype(jnp.bfloat16)
    paired_grad = jnp.concatenate([gate_grad, up_grad], axis=1)
    token_term = scale_in * jnp.dot(paired_grad, paired_weights, preferred_element_type=jnp.float32)
    token_grad = lax.psum_scatter(
        token_term.astype(jnp.bfloat16), "tensor", scatter_dimension=1, tiled=True
    )
    first_part = contract_rows(inputs, paired_grad)
    second_part = contract_rows(out_rows, hidden)
    summed = lax.psum_scatter(
        jnp.concatenate([first_part, second_part], axis=1).astype(jnp.bfloat16),
        "dp",
        scatter_dimension=0,
        tiled=True,
    ).astype(jnp.float32)
    sums = summed.T.reshape(3, width, columns)
    factors = jnp.array([scale_in, scale_in, scale_out], jnp.float32)
    gradient = sums * factors[:, None, None]
    new_first = beta_first * moment_first + (1.0 - beta_first) * gradient
    new_second = beta_second * moment_second + (1.0 - beta_second) * gradient * gradient
    first_hat = new_first / (1.0 - beta_first**step_power)
    second_hat = new_second / (1.0 - beta_second**step_power)
    update = first_hat / (jnp.sqrt(second_hat) + epsilon) + weight_decay * master
    weight_squares = jnp.sum(master * master, axis=(1, 2))
    update_squares = jnp.sum(update * update, axis=(1, 2))
    weight_part, update_part = lax.psum((weight_squares, update_squares), "tensor")
    weight_total, update_total = lax.psum((weight_part, update_part), "dp")
    trust_ratio = jnp.sqrt(weight_total) / jnp.sqrt(update_total)
    return (token_grad, trust_ratio[:, None, None] * update)


def solution(mesh):
    placed = (
        P("dp", "tensor"),
        P("dp", "tensor"),
        P(None, "tensor", "dp"),
        P(None, "tensor", "dp"),
        P(None, "tensor", "dp"),
    )
    return jax.shard_map(
        local,
        mesh=mesh,
        in_specs=placed,
        out_specs=(P("dp", "tensor"), P(None, "tensor", "dp")),
        check_vma=False,
    )
```

profile of v0, /device:TPU:16, one launch (start us, length us, event | category | flops | bytes accessed | tf_op | source)
XLA Modules:
  0.0 618.6 jit_solution(11447558265337889109)
XLA Ops:
  7.2 0.0 all-gather.6.cloned.1.call-start
  7.2 4.4 multiply_reduce_fusion.1
  11.6 0.0 all-gather.6.cloned.1.call-update
  11.6 0.0 all-gather.8.cloned.1.call-start
  11.7 0.7 all-gather.8.cloned.1.call-update
  12.4 0.0 all-gather.4.cloned.1.call-start
  12.4 0.7 all-gather.4.cloned.1.call-update
  13.1 0.0 reduce-scatter.7.cloned.1.call-start
  13.1 146.8 %all-gather.6.cloned.1.call-done = bf16[3,400,5120]{2,1,0:T(8,128)(2,1)} async-done(((bf16[3,400,640]{2,1,0:T(8,128)(2,1)}), bf16[3,400,5120]{2,1,0:T(8,128)(2,1)}) %all-gather.6.cloned.1.call-update) | async-done | bytes 12288016 | tf_op jit(solution)/shard_map/all_gather | solution.py:37
  159.9 7.0 %slice.17 = bf16[2,400,5120]{2,1,0:T(8,128)(2,1)} slice(bf16[3,400,5120]{2,1,0:T(8,128)(2,1)} %all-gather.6.cloned.1.call-done), slice={[0:2], [0:400], [0:5120]} | slice | bytes 16384000 | tf_op jit(solution)/shard_map/slice | solution.py:38
  166.9 59.8 %all-gather.8.cloned.1.call-done = bf16[256,5120]{0,1:T(8,128)(2,1)} async-done(((bf16[256,160]{0,1:T(8,128)(2,1)}), bf16[256,5120]{0,1:T(8,128)(2,1)}) %all-gather.8.cloned.1.call-update) | async-done | bytes 2621456 | tf_op jit(solution)/shard_map/all_gather | solution.py:33
  226.7 6.3 %convolution_multiply_fusion.1 = f32[256,800]{0,1:T(8,128)S(1)} fusion(bf16[800,5120]{1,0:T(8,128)(2,1)} %bitcast.23, bf16[256,5120]{0,1:T(8,128)(2,1)} %all-gather.8.cloned.1.call-done), kind=kOutput, calls=%fused_computation.19 | convolution fusion | flops 2097356800 | bytes 11632640 | tf_op jit(solution)/shard_map/dot_general | solution.py:16
  233.1 60.8 %all-gather.4.cloned.1.call-done = bf16[256,5120]{0,1:T(8,128)(2,1)} async-done(((bf16[256,160]{0,1:T(8,128)(2,1)}), bf16[256,5120]{0,1:T(8,128)(2,1)}) %all-gather.4.cloned.1.call-update) | async-done | bytes 2621456 | tf_op jit(solution)/shard_map/all_gather | solution.py:34
  293.8 0.0 copy-start.2
  293.8 4.4 multiply_convert_fusion.2
  298.2 0.0 copy-done.2
  298.2 0.0 copy-start.1
  298.2 1.3 fusion.1
  299.5 0.4 copy-done.1
  300.0 2.3 fusion
  302.3 10.4 %pad_maximum_fusion = bf16[5120,1200]{0,1:T(8,128)(2,1)} fusion(bf16[5120,400]{0,1:T(8,128)(2,1)S(1)} %fusion.1, bf16[5120,800]{0,1:T(8,128)(2,1)S(1)} %fusion), kind=kLoop, calls=%fused_computation | loop fusion | flops 24576000 | bytes 24576000 | tf_op jit(solution)/shard_map/concatenate | solution.py:58
  312.7 17.4 %copy.8 = bf16[5120,1200]{1,0:T(8,128)(2,1)} copy(bf16[5120,1200]{0,1:T(8,128)(2,1)} %pad_maximum_fusion) | data formatting | bytes 24576000
  330.1 0.0 reduce-scatter.7.cloned.1.call-update
  330.1 0.2 reduce-scatter.5.cloned.1.call-start
  330.3 8.7 %fusion.2 = bf16[256,5120]{0,1:T(8,128)(2,1)} fusion(bf16[800,5120]{1,0:T(8,128)(2,1)} %bitcast.24, bf16[256,400]{0,1:T(8,128)(2,1)S(1)} %get-tuple-element.11, bf16[256,400]{0,1:T(8,128)(2,1)S(1)} %get-tuple-element.10), kind=kOutput, calls=%fused_computation.6 | convolution fusion | flops 2100592640 | bytes 11223040 | tf_op jit(solution)/shard_map/dot_general | solution.py:51
  339.0 0.0 reduce-scatter.5.cloned.1.call-update
  339.0 150.4 %reduce-scatter.7.cloned.1.call-done = bf16[640,1200]{1,0:T(8,128)(2,1)} async-done(((bf16[5120,1200]{1,0:T(8,128)(2,1)}), bf16[640,1200]{1,0:T(8,128)(2,1)}) %reduce-scatter.7.cloned.1.call-update) | async-done | bytes 1536016
  489.4 2.7 copy.9
  492.1 0.0 copy-start
  492.1 0.0 copy-start.3
  492.1 0.2 reshape.20
  492.3 1.6 copy-done
  494.0 0.0 copy-done.3
  494.0 5.4 multiply_reduce_fusion
  499.4 55.1 %all-reduce = (f32[3]{0:T(128)S(1)}, f32[3]{0:T(128)S(1)}) all-reduce(f32[3]{0:T(128)S(1)} %get-tuple-element.6, f32[3]{0:T(128)S(1)} %get-tuple-element.8), channel_id=1, replica_groups=mesh['dp'=8,'tensor'=32] {'tensor'}, use_global_device_ids=true, to_apply=%region_6.0 | all-reduce | flops 6 | bytes 48 | tf_op jit(solution)/shard_map/psum | solution.py:73
  554.5 19.3 %all-reduce.1 = (f32[3]{0:T(128)S(1)}, f32[3]{0:T(128)S(1)}) all-reduce(f32[3]{0:T(128)S(1)} %get-tuple-element.2, f32[3]{0:T(128)S(1)} %get-tuple-element.3), channel_id=1, replica_groups=mesh['dp'=8,'tensor'=32] {'dp'}, use_global_device_ids=true, to_apply=%region_7.0 | all-reduce | flops 6 | bytes 48 | tf_op jit(solution)/shard_map/psum | solution.py:74
  573.8 1.9 broadcast_multiply_fusion
  575.7 36.3 %reduce-scatter.5.cloned.1.call-done = bf16[256,160]{0,1:T(8,128)(2,1)} async-done(((bf16[256,5120]{0,1:T(8,128)(2,1)}), bf16[256,160]{0,1:T(8,128)(2,1)}) %reduce-scatter.5.cloned.1.call-update) | async-done | bytes 81936 | tf_op jit(solution)/shard_map/reduce_scatter | solution.py:52
  (1 shorter events, 0.0 us)
Async XLA Ops:
  7.2 152.7 %all-gather.6.cloned.1.call-start = ((), (), s32[]{:S(2)}) async-start(), calls=%async_computation.3 | async-start | bytes 13824000 | tf_op jit(solution)/shard_map/all_gather | solution.py:37
  11.6 215.1 %all-gather.8.cloned.1.call-start = ((), (), s32[]{:S(2)}) async-start(), calls=%async_computation.4 | async-start | bytes 2703360 | tf_op jit(solution)/shard_map/all_gather | solution.py:33
  12.4 281.5 %all-gather.4.cloned.1.call-start = ((), (), s32[]{:S(2)}) async-start(), calls=%async_computation.2 | async-start | bytes 2703360 | tf_op jit(solution)/shard_map/all_gather | solution.py:34
  13.1 476.3 %reduce-scatter.7.cloned.1.call-start = ((), (), s32[]{:S(2)}) async-start(), calls=%async_computation.6 | async-start | bytes 14745600
  293.8 4.4 copy-start.2
  298.2 1.7 copy-start.1
  330.1 282.0 %reduce-scatter.5.cloned.1.call-start = ((), (), s32[]{:S(2)}) async-start(), calls=%async_computation.5 | async-start | bytes 2703360 | tf_op jit(solution)/shard_map/reduce_scatter | solution.py:52
  492.1 1.9 copy-start
  492.1 1.9 copy-start.3
Sparse Core Ops, SparseCore 0:
  11.7 148.1 all-gather.5
  161.8 64.9 all-gather.7
  228.6 65.1 all-gather.3
  330.2 159.1 reduce-scatter.6
  492.4 119.6 reduce-scatter.4
where the time goes:
time: 619 us
  waiting for transfers between devices  455 us (74%)
  blocking collectives  74.4 us (12%)
  local copies, waits for them, and re-layouts  29.2 us (5%)
  matrix products  23 us (4%)
  other arithmetic  22.2 us (4%)
  between operations  13.9 us (2%)
    unnamed x6, waiting for transfers between devices  152 us
    all_gather x1, waiting for transfers between devices, local(): weights = lax.all_gather(local_weights, 'dp', axis=2, tiled=True)  147 us
    all_gather x1, waiting for transfers between devices, local(): lax.all_gather(out_grad, 'tensor', axis=1, tiled=True)  60.8 us
    all_gather x1, waiting for transfers between devices, local(): lax.all_gather(tokens, 'tensor', axis=1, tiled=True)  59.8 us
    psum x1, blocking collectives, local(): lax.psum((weight_squares, update_squares), 'tensor')  55.1 us
    reduce_scatter x1, waiting for transfers between devices, local(): lax.psum_scatter(token_term.astype(jnp.bfloat16), 'tensor', scatter_dimen...  36.3 us
    unnamed x10, local copies, waits for them, and re-layouts  22.2 us
    psum x1, blocking collectives, local(): weight_total, update_total = lax.psum((weight_part, update_part), 'dp')  19.3 us
  transfers between devices with their start and end apart: 5, of which 5 were waited for; matrix products, arithmetic and copies ran while one was open for 5% of the time, Pallas kernels for 0%

commit v1 on v0

--- a/solution.py
+++ b/solution.py
@@ -34,7 +34,9 @@
         lax.all_gather(out_grad, "tensor", axis=1, tiled=True),
     )
     local_weights = master.astype(jnp.bfloat16)
-    weights = lax.all_gather(local_weights, "dp", axis=2, tiled=True)
+    weights = jnp.concatenate(
+        lax.all_to_all(jnp.stack([local_weights] * lax.axis_size("dp")), "dp", 0, 0), axis=2
+    )
     paired_weights = weights[:2].reshape(2 * width, weights.shape[2])
     both_pre = scale_in * contract_last(inputs, paired_weights)
     gate_pre = both_pre[:, :width]

time: 619 us -> 539 us (0.87)
  waiting for transfers between devices: 455 us -> 347 us
  local copies, waits for them, and re-layouts: 29.2 us -> 51.8 us
  starting transfers between devices: 0.38 us -> 7.4 us
    all_to_all x0 -> x1, waiting for transfers between devices: none -> 160 us  [local(): lax.all_to_all(jnp.stack([local_weights] * lax.axis_size('dp')), 'dp', 0, 0)]
    all_gather x1 -> x0, waiting for transfers between devices: 147 us -> none  [local(): weights = lax.all_gather(local_weights, 'dp', axis=2, tiled=True)]
    all_gather x1, waiting for transfers between devices: 60.8 us -> 0.02 us  [local(): lax.all_gather(out_grad, 'tensor', axis=1, tiled=True)]
    all_gather x1, waiting for transfers between devices: 59.8 us -> 0.01 us  [local(): lax.all_gather(tokens, 'tensor', axis=1, tiled=True)]
    unnamed x10 -> x15, local copies, waits for them, and re-layouts: 22.2 us -> 32.9 us
    all_to_all x0 -> x1, starting transfers between devices: none -> 7.28 us  [local(): lax.all_to_all(jnp.stack([local_weights] * lax.axis_size('dp')), 'dp', 0, 0)]
    slice x1 -> x2, local copies, waits for them, and re-layouts: 7.03 us -> 13.4 us  [local(): paired_weights = weights[:2].reshape(2 * width, weights.shape[2])]
    unnamed x6 -> x5, waiting for transfers between devices: 152 us -> 151 us
  transfers between devices with their start and end apart: 5 -> 5, of which waited for: 5 -> 3; matrix products, arithmetic and copies ran while one was open for 5% -> 9% of each run, Pallas kernels for 0% -> 0%
where the time goes in v1:
time: 539 us; the launch traced here: 538 us
  waiting for transfers between devices  347 us (64%)
  blocking collectives  74.6 us (14%)
  local copies, waits for them, and re-layouts  51.8 us (10%)
  matrix products  22 us (4%)
  other arithmetic  21.1 us (4%)
  between operations  13.9 us (3%)
  starting transfers between devices  7.4 us (1%)
    all_to_all x1, waiting for transfers between devices, local(): lax.all_to_all(jnp.stack([local_weights] * lax.axis_size('dp')), 'dp', 0, 0)  160 us
    unnamed x5, waiting for transfers between devices  151 us
    psum x1, blocking collectives, local(): lax.psum((weight_squares, update_squares), 'tensor')  55.3 us
    reduce_scatter x1, waiting for transfers between devices, local(): lax.psum_scatter(token_term.astype(jnp.bfloat16), 'tensor', scatter_dimen...  35.9 us
    unnamed x15, local copies, waits for them, and re-layouts  32.9 us
    psum x1, blocking collectives, local(): weight_total, update_total = lax.psum((weight_part, update_part), 'dp')  19.3 us
    slice x2, local copies, waits for them, and re-layouts, local(): paired_weights = weights[:2].reshape(2 * width, weights.shape[2])  13.4 us
  transfers between devices with their start and end apart: 5, of which 3 were waited for; matrix products, arithmetic and copies ran while one was open for 9% of the time, Pallas kernels for 0%

profile of v1, /device:TPU:16, one launch (start us, length us, event | category | flops | bytes accessed | tf_op | source)
XLA Modules:
  0.0 537.6 jit_solution(13276983271528284970)
XLA Ops:
  7.2 3.3 multiply_reduce_fusion.1
  10.4 5.5 %stack.2 = bf16[8,3,400,640]{3,2,1,0:T(8,128)(2,1)} broadcast(bf16[3,400,640]{2,1,0:T(8,128)(2,1)S(1)} %get-tuple-element.9), dimensions={1,2,3} | broadcast | bytes 13824000 | tf_op jit(solution)/shard_map/stack | solution.py:38
  15.9 7.3 %all-to-all-start = ((bf16[8,3,400,640]{3,2,1,0:T(8,128)(2,1)}), bf16[8,3,400,640]{3,2,1,0:T(8,128)(2,1)}, u32[]{:S(2)}, u32[]{:S(2)}) async-start(bf16[8,3,400,640]{3,2,1,0:T(8,128)(2,1)} %stack.2), calls=%async_computation | async-start | bytes 24576000 | tf_op jit(solution)/shard_map/all_to_all | solution.py:38
  23.2 0.0 all-gather.5.cloned.1.call-start
  23.2 0.7 all-gather.5.cloned.1.call-update
  23.9 0.0 all-gather.3.cloned.1.call-start
  23.9 0.7 all-gather.3.cloned.1.call-update
  24.6 0.0 reduce-scatter.7.cloned.1.call-start
  24.7 159.9 %all-to-all-done = bf16[8,3,400,640]{3,2,1,0:T(8,128)(2,1)} async-done(((bf16[8,3,400,640]{3,2,1,0:T(8,128)(2,1)}), bf16[8,3,400,640]{3,2,1,0:T(8,128)(2,1)}, u32[]{:S(2)}, u32[]{:S(2)}) %all-to-all-start) | async-done | bytes 12288032 | tf_op jit(solution)/shard_map/all_to_all | solution.py:38
  184.6 7.2 %slice.19 = bf16[2,400,8,640]{3,1,0,2:T(8,128)(2,1)} slice(bf16[3,400,8,640]{3,1,0,2:T(8,128)(2,1)} %bitcast), slice={[0:2], [0:400], [0:8], [0:640]} | slice | bytes 16384000 | tf_op jit(solution)/shard_map/slice | solution.py:40
  191.7 6.2 %copy.9 = bf16[2,400,8,640]{3,2,1,0:T(8,128)(2,1)S(1)} copy(bf16[2,400,8,640]{3,1,0,2:T(8,128)(2,1)} %slice.19) | data formatting | bytes 16384000 | tf_op jit(solution)/shard_map/slice | solution.py:40
  198.0 5.1 copy.13
  203.1 2.5 slice_bitcast_fusion
  205.6 2.6 copy.12
  208.2 0.0 all-gather.5.cloned.1.call-done
  208.2 6.3 %convolution_multiply_fusion.1 = f32[256,800]{0,1:T(8,128)S(1)} fusion(bf16[800,5120]{1,0:T(8,128)(2,1)} %bitcast.26, bf16[256,5120]{0,1:T(8,128)(2,1)} %all-gather.5.cloned.1.call-done), kind=kOutput, calls=%fused_computation.17 | convolution fusion | flops 2097356800 | bytes 11632640 | tf_op jit(solution)/shard_map/dot_general | solution.py:16
  214.5 0.0 all-gather.3.cloned.1.call-done
  214.5 0.0 copy-start.1
  214.5 0.0 copy-start.3
  214.6 3.2 fusion.1
  217.7 0.0 copy-done.1
  217.7 0.6 copy-done.3
  218.3 0.0 copy-start.2
  218.3 1.3 multiply_convert_fusion.2
  219.6 0.5 copy-done.2
  220.1 2.5 fusion
  222.6 10.3 %pad_maximum_fusion = bf16[5120,1200]{0,1:T(8,128)(2,1)} fusion(bf16[5120,400]{0,1:T(8,128)(2,1)S(1)} %fusion.1, bf16[5120,800]{0,1:T(8,128)(2,1)S(1)} %fusion), kind=kLoop, calls=%fused_computation | loop fusion | flops 24576000 | bytes 24576000 | tf_op jit(solution)/shard_map/concatenate | solution.py:60
  232.9 17.3 %copy.10 = bf16[5120,1200]{1,0:T(8,128)(2,1)} copy(bf16[5120,1200]{0,1:T(8,128)(2,1)} %pad_maximum_fusion) | data formatting | bytes 24576000
  250.2 0.0 reduce-scatter.7.cloned.1.call-update
  250.2 0.0 reduce-scatter.5.cloned.1.call-start
  250.3 8.7 %fusion.2 = bf16[256,5120]{0,1:T(8,128)(2,1)} fusion(bf16[800,5120]{1,0:T(8,128)(2,1)} %bitcast.27, bf16[256,400]{0,1:T(8,128)(2,1)S(1)} %get-tuple-element.11, bf16[256,400]{0,1:T(8,128)(2,1)S(1)} %get-tuple-element.10), kind=kOutput, calls=%fused_computation.6 | convolution fusion | flops 2100592640 | bytes 11223040 | tf_op jit(solution)/shard_map/dot_general | solution.py:53
  259.0 0.0 reduce-scatter.5.cloned.1.call-update
  259.0 149.7 %reduce-scatter.7.cloned.1.call-done = bf16[640,1200]{1,0:T(8,128)(2,1)} async-done(((bf16[5120,1200]{1,0:T(8,128)(2,1)}), bf16[640,1200]{1,0:T(8,128)(2,1)}) %reduce-scatter.7.cloned.1.call-update) | async-done | bytes 1536016
  408.7 2.7 copy.11
  411.4 0.0 copy-start
  411.4 0.0 copy-start.4
  411.4 0.2 reshape.31
  411.7 1.6 copy-done
  413.3 0.0 copy-done.4
  413.3 5.4 %multiply_reduce_fusion = (f32[3]{0:T(128)S(1)}, f32[3,400,640]{2,1,0:T(8,128)S(1)}) fusion(f32[3,400,640]{2,1,0:T(8,128)S(1)} %copy-done, f32[3,400,640]{2,1,0:T(8,128)} %param.10, f32[3,400,640]{2,1,0:T(8,128)S(1)} %bitcast.25, f32[3]{0:T(128)S(1)} %copy-done.4, f32[3,400,640]{2,1,0:T(8,128)} %param.9), kind=kLoop, calls=%fused_computation.14 | loop fusion | flops 12287997 | bytes 15360024 | tf_op jit(solution)/shard_map/reduce_sum | solution.py:74
  418.7 55.3 %all-reduce = (f32[3]{0:T(128)S(1)}, f32[3]{0:T(128)S(1)}) all-reduce(f32[3]{0:T(128)S(1)} %get-tuple-element.6, f32[3]{0:T(128)S(1)} %get-tuple-element.8), channel_id=1, replica_groups=mesh['dp'=8,'tensor'=32] {'tensor'}, use_global_device_ids=true, to_apply=%region_6.0 | all-reduce | flops 6 | bytes 48 | tf_op jit(solution)/shard_map/psum | solution.py:75
  474.0 19.3 %all-reduce.1 = (f32[3]{0:T(128)S(1)}, f32[3]{0:T(128)S(1)}) all-reduce(f32[3]{0:T(128)S(1)} %get-tuple-element.2, f32[3]{0:T(128)S(1)} %get-tuple-element.3), channel_id=1, replica_groups=mesh['dp'=8,'tensor'=32] {'dp'}, use_global_device_ids=true, to_apply=%region_7.0 | all-reduce | flops 6 | bytes 48 | tf_op jit(solution)/shard_map/psum | solution.py:76
  493.3 1.9 broadcast_multiply_fusion
  495.2 35.9 %reduce-scatter.5.cloned.1.call-done = bf16[256,160]{0,1:T(8,128)(2,1)} async-done(((bf16[256,5120]{0,1:T(8,128)(2,1)}), bf16[256,160]{0,1:T(8,128)(2,1)}) %reduce-scatter.5.cloned.1.call-update) | async-done | bytes 81936 | tf_op jit(solution)/shard_map/reduce_scatter | solution.py:54
  (1 shorter events, 0.0 us)
Async XLA Ops:
  15.9 168.7 %all-to-all-start = ((bf16[8,3,400,640]{3,2,1,0:T(8,128)(2,1)}), bf16[8,3,400,640]{3,2,1,0:T(8,128)(2,1)}, u32[]{:S(2)}, u32[]{:S(2)}) async-start(bf16[8,3,400,640]{3,2,1,0:T(8,128)(2,1)} %stack.2), calls=%async_computation | async-start | bytes 24576000 | tf_op jit(solution)/shard_map/all_to_all | solution.py:38
  23.2 185.0 %all-gather.5.cloned.1.call-start = ((), (), s32[]{:S(2)}) async-start(), calls=%async_computation.4 | async-start | bytes 2703360 | tf_op jit(solution)/shard_map/all_gather | solution.py:33
  23.9 190.6 %all-gather.3.cloned.1.call-start = ((), (), s32[]{:S(2)}) async-start(), calls=%async_computation.3 | async-start | bytes 2703360 | tf_op jit(solution)/shard_map/all_gather | solution.py:34
  24.6 384.1 %reduce-scatter.7.cloned.1.call-start = ((), (), s32[]{:S(2)}) async-start(), calls=%async_computation.6 | async-start | bytes 14745600
  214.5 3.2 copy-start.1
  214.5 3.8 copy-start.3
  218.3 1.7 copy-start.2
  250.2 280.8 %reduce-scatter.5.cloned.1.call-start = ((), (), s32[]{:S(2)}) async-start(), calls=%async_computation.5 | async-start | bytes 2703360 | tf_op jit(solution)/shard_map/reduce_scatter | solution.py:54
  411.4 1.9 copy-start
  411.4 1.9 copy-start.4
Sparse Core Ops, SparseCore 0:
  25.9 68.3 all-gather.4
  96.1 64.9 all-gather.2
  250.4 158.3 reduce-scatter.6
  411.7 119.3 reduce-scatter.4
